TPU v7x, 1024 devices: a whole 8x8x8 slice. The times are simulated.
1024 devices in a mesh: section: 8 (over y), seq: 8 (over z), dp: 16 (over x, core).
Axes of the slice: x: 8, y: 8, z: 8, core: 2. Of those that a mesh axis runs over, the one named last changes fastest.
Arguments:
- section_inputs: bfloat16 [8, 16, 1024, 2560], P('section', 'dp', 'seq'), may hold values from -6 to 6
- grad_send: bfloat16 [8, 16, 1024, 2560], P('section', 'dp', 'seq'), may hold values from -6 to 6
- gains: float32 [8, 3, 2560], P('section'), may hold values from -6 to 6
- layout: int32 [8, 8], P('section', 'seq'), may hold values 0 or 1
Outputs:
- input_grad: bfloat16 [8, 16, 1024, 2560], P('section', 'dp', 'seq')
- gain_grads: float32 [8, 3, 2560], P('section')
All inputs are finite; a program needn't handle non-finite values. No bound on the sum of `layout` on one device may be relied on, other than what follows from the above.
Results may differ from a plain program's by a relative error of at most 0.02.
Values may be sent and summed in bfloat16 or wider, within the bound.
A program may use at most 32 MiB of HBM per device.

v0:
```python
import math

import jax
import jax.numpy as jnp
from jax import lax
from jax.sharding import PartitionSpec as P

HEAD_DIM = 128


EPS = 1e-06
NEG = -1e30


def shifted(block, axis, distance):
    devices = range(lax.axis_size(axis))
    route = [((i - distance) % len(devices), i) for i in devices]
    return lax.ppermute(block, axis, route)


def from_behind(value, axis, steps):
    count = lax.axis_size(axis)
    initial, last = (max(0, -steps), min(count, count - steps))
    return lax.ppermute(value, axis, [(source, source + steps) for source in range(initial, last)])


def contract(form, left, right):
    return jnp.einsum(form, left, right, preferred_element_type=jnp.float32)


def normalize(inputs):
    input_float = inputs.astype(jnp.float32)
    scale_inv = lax.rsqrt(jnp.mean(input_float * input_float, axis=-1, keepdims=True) + EPS)
    return ((input_float * scale_inv).astype(jnp.bfloat16), scale_inv)


def project(normed, gain_row):
    return (normed.astype(jnp.float32) * gain_row).astype(jnp.bfloat16)


def heads_of(tensor, head_dim):
    return tensor.reshape(tensor.shape[0], tensor.shape[1], tensor.shape[2] // head_dim, head_dim)


def flatten(tensor):
    return tensor.reshape(tensor.shape[0], tensor.shape[1], tensor.shape[2] * tensor.shape[3])


def weights_of(query_heads, key_heads, far_key_heads, usable, head_dim):
    factor = 1.0 / math.sqrt(head_dim)
    near_scores = contract("nthe,nuhe->nhtu", query_heads, key_heads) * factor
    far_scores = contract("nthe,nuhe->nhtu", query_heads, far_key_heads) * factor
    row_index = lax.broadcasted_iota(jnp.int32, near_scores.shape[-2:], 0)
    col_index = lax.broadcasted_iota(jnp.int32, near_scores.shape[-2:], 1)
    near_scores = jnp.where(row_index >= col_index, near_scores, NEG)
    far_scores = jnp.where(usable[:, None, None, None], far_scores, NEG)
    row_top = jnp.maximum(
        jnp.max(near_scores, axis=-1, keepdims=True), jnp.max(far_scores, axis=-1, keepdims=True)
    )
    near_exp = jnp.exp(near_scores - row_top)
    far_exp = jnp.exp(far_scores - row_top)
    row_total = jnp.sum(near_exp, axis=-1, keepdims=True) + jnp.sum(far_exp, axis=-1, keepdims=True)
    return (near_exp / row_total, far_exp / row_total)


def attention_grads(
    queries, keys_own, values_own, keys_far, values_far, grad_out, usable, head_dim
):
    query_heads = heads_of(queries, head_dim)
    key_heads = heads_of(keys_own, head_dim)
    value_heads = heads_of(values_own, head_dim)
    far_key_heads = heads_of(keys_far, head_dim)
    far_value_heads = heads_of(values_far, head_dim)
    grad_heads = heads_of(grad_out, head_dim)
    near_prob, far_prob = weights_of(query_heads, key_heads, far_key_heads, usable, head_dim)
    near_dprob = contract("nthe,nuhe->nhtu", grad_heads, value_heads)
    far_dprob = contract("nthe,nuhe->nhtu", grad_heads, far_value_heads)
    row_delta = jnp.sum(near_prob * near_dprob, axis=-1, keepdims=True) + jnp.sum(
        far_prob * far_dprob, axis=-1, keepdims=True
    )
    factor = 1.0 / math.sqrt(head_dim)
    near_dscore = (near_prob * (near_dprob - row_delta) * factor).astype(jnp.bfloat16)
    far_dscore = (far_prob * (far_dprob - row_delta) * factor).astype(jnp.bfloat16)
    d_query = contract("nhtu,nuhe->nthe", near_dscore, key_heads) + contract(
        "nhtu,nuhe->nthe", far_dscore, far_key_heads
    )
    d_key_own = contract("nhtu,nthe->nuhe", near_dscore, query_heads)
    d_key_far = contract("nhtu,nthe->nuhe", far_dscore, query_heads).astype(jnp.bfloat16)
    d_value_own = contract("nhtu,nthe->nuhe", near_prob.astype(jnp.bfloat16), grad_heads)
    d_value_far = contract("nhtu,nthe->nuhe", far_prob.astype(jnp.bfloat16), grad_heads).astype(
        jnp.bfloat16
    )
    return (
        flatten(d_query),
        flatten(d_key_own),
        flatten(d_value_own),
        flatten(d_key_far),
        flatten(d_value_far),
    )


def finish(inputs, normed, scale_inv, grad_out, d_query, d_key, d_value, gain_rows):
    d_normed = d_query * gain_rows[0] + d_key * gain_rows[1] + d_value * gain_rows[2]
    input_float = inputs.astype(jnp.float32)
    input_grad = (
        grad_out.astype(jnp.float32)
        + scale_inv * d_normed
        - input_float * scale_inv**3 * jnp.mean(d_normed * input_float, axis=-1, keepdims=True)
    ).astype(jnp.bfloat16)
    normed_float = normed.astype(jnp.float32)
    terms = jnp.stack(
        [
            jnp.sum(d_query * normed_float, axis=(0, 1)),
            jnp.sum(d_key * normed_float, axis=(0, 1)),
            jnp.sum(d_value * normed_float, axis=(0, 1)),
        ]
    )
    return (input_grad, terms)


def local(section_inputs, grad_send, gains, layout):
    head_dim = HEAD_DIM
    inputs = section_inputs[0]
    grad_out = shifted(grad_send[0], "section", -1)
    gain_rows = gains[0]
    stride = lax.axis_size("seq") // 2
    usable = (lax.axis_index("seq") >= stride) & (layout[0, 0] == 1)
    usable = jnp.broadcast_to(usable, (inputs.shape[0],))
    normed, scale_inv = normalize(inputs)
    queries = project(normed, gain_rows[0])
    keys_own = project(normed, gain_rows[1])
    values_own = project(normed, gain_rows[2])
    keys_far, values_far = from_behind((keys_own, values_own), "seq", stride)
    grads = attention_grads(
        queries, keys_own, values_own, keys_far, values_far, grad_out, usable, head_dim
    )
    key_back, value_back = from_behind((grads[3], grads[4]), "seq", -stride)
    d_key = grads[1] + key_back.astype(jnp.float32)
    d_value = grads[2] + value_back.astype(jnp.float32)
    input_grad, terms = finish(
        inputs, normed, scale_inv, grad_out, grads[0], d_key, d_value, gain_rows
    )
    summed = lax.psum(terms, ("seq", "dp"))
    tokens_all = inputs.shape[0] * inputs.shape[1] * lax.axis_size("dp") * lax.axis_size("seq")
    gain_grads = summed / math.sqrt(tokens_all)
    return (input_grad[None], gain_grads[None])


def solution(mesh):
    in_specs = (
        P("section", "dp", "seq", None),
        P("section", "dp", "seq", None),
        P("section", None, None),
        P("section", "seq"),
    )
    out_specs = (P("section", "dp", "seq", None), P("section", None, None))
    return jax.shard_map(local, mesh=mesh, in_specs=in_specs, out_specs=out_specs, check_vma=False)
```

profile of v0, /device:TPU:1, one launch (start us, length us, event | category | flops | bytes accessed | tf_op | source)
XLA Modules:
  0.0 609.0 jit_solution(12929392180638478619)
XLA Ops:
  0.6 0.0 copy-start.1
  0.6 2.2 copy.26
  2.9 0.0 copy-start.2
  2.9 6.8 %collective-permute-start = (bf16[1,128,2560]{1,2,0:T(8,128)(2,1)}, bf16[1,128,2560]{1,2,0:T(8,128)(2,1)S(1)}, u32[]{:S(2)}, u32[]{:S(2)}) collective-permute-start(bf16[1,128,2560]{1,2,0:T(8,128)(2,1)} %bitcast), channel_id=1, source_target_pairs={{128,0},{256,128},{384,256},{512,384},{640,512},{768,640},{896,768... | collective-permute-start | bytes 1966088 | tf_op jit(solution)/shard_map/ppermute | solution.py:18
  9.7 0.0 copy-done.1
  9.7 0.3 copy.27
  10.1 0.4 fusion.12
  10.4 0.0 copy-done.2
  10.4 0.1 slice_reduce_fusion.1
  10.5 2.2 fusion.5
  12.8 15.1 %collective-permute-start.1 = (bf16[1,128,2560]{1,2,0:T(8,128)(2,1)}, bf16[1,128,2560]{1,2,0:T(8,128)(2,1)}, u32[]{:S(2)}, u32[]{:S(2)}) collective-permute-start(bf16[1,128,2560]{1,2,0:T(8,128)(2,1)} %get-tuple-element.15), channel_id=1, source_target_pairs={{0,64},{16,80},{32,96},{48,112},{1,65},{17,81},{33,97},{49,113},{2... | collective-permute-start | bytes 1966088 | tf_op jit(solution)/shard_map/ppermute | solution.py:24
  27.9 2.1 collective-permute-start.2
  30.0 0.1 convert_element_type.269
  30.1 0.2 multiply_convert_fusion.3
  30.3 2.3 fusion.39
  33.3 7.1 %collective-permute-done.1 = bf16[1,128,2560]{1,2,0:T(8,128)(2,1)} collective-permute-done((bf16[1,128,2560]{1,2,0:T(8,128)(2,1)}, bf16[1,128,2560]{1,2,0:T(8,128)(2,1)}, u32[]{:S(2)}, u32[]{:S(2)}) %collective-permute-start.1) | collective-permute-done | bytes 655392 | tf_op jit(solution)/shard_map/ppermute | solution.py:24
  40.4 0.0 copy-start
  40.4 2.0 fusion.40
  42.4 0.0 copy-done
  42.4 0.5 fusion.21
  42.9 0.0 collective-permute-done
  42.9 1.1 convolution_bitcast_fusion.1
  44.0 0.6 convolution_convert_fusion
  44.6 9.8 %collective-permute-done.2 = bf16[1,128,2560]{1,2,0:T(8,128)(2,1)} collective-permute-done((bf16[1,128,2560]{1,2,0:T(8,128)(2,1)}, bf16[1,128,2560]{1,2,0:T(8,128)(2,1)}, u32[]{:S(2)}, u32[]{:S(2)}) %collective-permute-start.2) | collective-permute-done | bytes 655392 | tf_op jit(solution)/shard_map/ppermute | solution.py:24
  54.5 1.9 multiply_reduce_fusion
  56.3 0.8 multiply_convert_fusion.2
  57.1 0.5 convolution_convert_fusion.1
  57.7 1.3 collective-permute-start.3
  59.0 1.3 collective-permute-start.4
  60.3 0.8 fusion.28
  61.0 1.7 fusion.11
  62.8 0.8 fusion.32
  63.5 0.6 fusion.25
  64.1 39.5 %collective-permute-done.3 = bf16[1,128,2560]{1,2,0:T(8,128)(2,1)S(1)} collective-permute-done((bf16[1,128,2560]{1,2,0:T(8,128)(2,1)S(1)}, bf16[1,128,2560]{1,2,0:T(8,128)(2,1)S(1)}, u32[]{:S(2)}, u32[]{:S(2)}) %collective-permute-start.3) | collective-permute-done | bytes 655392 | tf_op jit(solution)/shard_map/ppermute | solution.py:24
  103.7 14.0 %collective-permute-done.4 = bf16[1,128,2560]{1,2,0:T(8,128)(2,1)S(1)} collective-permute-done((bf16[1,128,2560]{1,2,0:T(8,128)(2,1)S(1)}, bf16[1,128,2560]{1,2,0:T(8,128)(2,1)S(1)}, u32[]{:S(2)}, u32[]{:S(2)}) %collective-permute-start.4) | collective-permute-done | bytes 655392 | tf_op jit(solution)/shard_map/ppermute | solution.py:24
  117.7 2.6 fusion.7
  120.4 0.4 fusion.22
  120.7 1.1 copy.42
  121.9 486.5 %psum.7 = f32[3,2560]{1,0:T(4,128)S(1)} all-reduce(f32[3,2560]{1,0:T(4,128)S(1)} %pad_maximum_fusion), channel_id=1, replica_groups=mesh['section'=8,'seq'=8,'dp'=16] {'seq','dp'}, use_global_device_ids=true, to_apply=%region_11.12 | all-reduce | flops 7680 | bytes 61440 | tf_op jit(solution)/shard_map/psum | solution.py:143
  608.4 0.6 broadcast_in_dim.36
  (11 shorter events, 0.1 us)
Async XLA Ops:
  0.6 9.1 %copy-start.1 = (bf16[1,1,128,2560]{3,2,1,0:T(8,128)(2,1)S(1)}, bf16[1,1,128,2560]{3,2,1,0:T(8,128)(2,1)}, u32[]{:S(2)}) copy-start(bf16[1,1,128,2560]{3,2,1,0:T(8,128)(2,1)} %param.4) | copy-start | bytes 1966084
  2.9 7.6 %copy-start.2 = (f32[1,3,2560]{2,0,1:T(1,128)S(1)}, f32[1,3,2560]{2,0,1:T(1,128)}, u32[]{:S(2)}) copy-start(f32[1,3,2560]{2,0,1:T(1,128)} %param.6) | copy-start | bytes 92164
  2.9 40.1 %collective-permute-start = (bf16[1,128,2560]{1,2,0:T(8,128)(2,1)}, bf16[1,128,2560]{1,2,0:T(8,128)(2,1)S(1)}, u32[]{:S(2)}, u32[]{:S(2)}) collective-permute-start(bf16[1,128,2560]{1,2,0:T(8,128)(2,1)} %bitcast), channel_id=1, source_target_pairs={{128,0},{256,128},{384,256},{512,384},{640,512},{768,640},{896,768... | collective-permute-start | bytes 1966088 | tf_op jit(solution)/shard_map/ppermute | solution.py:18
  12.8 27.6 %collective-permute-start.1 = (bf16[1,128,2560]{1,2,0:T(8,128)(2,1)}, bf16[1,128,2560]{1,2,0:T(8,128)(2,1)}, u32[]{:S(2)}, u32[]{:S(2)}) collective-permute-start(bf16[1,128,2560]{1,2,0:T(8,128)(2,1)} %get-tuple-element.15), channel_id=1, source_target_pairs={{0,64},{16,80},{32,96},{48,112},{1,65},{17,81},{33,97},{49,113},{2... | collective-permute-start | bytes 1966088 | tf_op jit(solution)/shard_map/ppermute | solution.py:24
  27.9 26.6 %collective-permute-start.2 = (bf16[1,128,2560]{1,2,0:T(8,128)(2,1)}, bf16[1,128,2560]{1,2,0:T(8,128)(2,1)}, u32[]{:S(2)}, u32[]{:S(2)}) collective-permute-start(bf16[1,128,2560]{1,2,0:T(8,128)(2,1)} %get-tuple-element.16), channel_id=1, source_target_pairs={{0,64},{16,80},{32,96},{48,112},{1,65},{17,81},{33,97},{49,113},{2... | collective-permute-start | bytes 1966088 | tf_op jit(solution)/shard_map/ppermute | solution.py:24
  40.4 2.0 copy-start
  57.7 46.0 %collective-permute-start.3 = (bf16[1,128,2560]{1,2,0:T(8,128)(2,1)S(1)}, bf16[1,128,2560]{1,2,0:T(8,128)(2,1)S(1)}, u32[]{:S(2)}, u32[]{:S(2)}) collective-permute-start(bf16[1,128,2560]{1,2,0:T(8,128)(2,1)S(1)} %bitcast.116), channel_id=1, source_target_pairs={{64,0},{80,16},{96,32},{112,48},{65,1},{81,17},{97,33},{113,49},{6... | collective-permute-start | bytes 1966088 | tf_op jit(solution)/shard_map/ppermute | solution.py:24
  59.0 58.8 %collective-permute-start.4 = (bf16[1,128,2560]{1,2,0:T(8,128)(2,1)S(1)}, bf16[1,128,2560]{1,2,0:T(8,128)(2,1)S(1)}, u32[]{:S(2)}, u32[]{:S(2)}) collective-permute-start(bf16[1,128,2560]{1,2,0:T(8,128)(2,1)S(1)} %bitcast.126), channel_id=1, source_target_pairs={{64,0},{80,16},{96,32},{112,48},{65,1},{81,17},{97,33},{113,49},{6... | collective-permute-start | bytes 1966088 | tf_op jit(solution)/shard_map/ppermute | solution.py:24
where the time goes:
time: 611 us; the launch traced here: 609 us
  blocking collectives  486 us (80%)
  waiting for transfers between devices  70.6 us (12%)
  starting transfers between devices  26.7 us (4%)
  matrix products  12.2 us (2%)
  other arithmetic  7.19 us (1%)
    psum x1, blocking collectives, local(): summed = lax.psum(terms, ('seq', 'dp'))  486 us
    ppermute x4, waiting for transfers between devices, from_behind(): lax.ppermute(value, axis, [(source, source + steps) for source in range(i...  70.6 us
    ppermute x4, starting transfers between devices, from_behind(): lax.ppermute(value, axis, [(source, source + steps) for source in range(i...  19.8 us
  transfers between devices with their start and end apart: 5, of which 4 were waited for; matrix products, arithmetic and copies ran while one was open for 2% of the time, Pallas kernels for 0%

commit v1 on v0

v1 whole, which is shorter than its diff:
```python
import math

import jax
import jax.numpy as jnp
from jax import lax
from jax.experimental import pallas as pl
from jax.experimental.pallas import tpu as pltpu
from jax.sharding import PartitionSpec as P

MESH = pl.DeviceIdType.MESH
HEAD = 128
EPS = 1e-06
NEG = -1e30
PER = 2
F32 = jnp.float32
BF16 = jnp.bfloat16


def dot(left, right, dims):
    return lax.dot_general(left, right, (dims, ((), ())), preferred_element_type=F32)


def make_kernel(n_seq, n_dp, n_section, channels, block):
    heads = channels // HEAD
    chunks = heads // PER
    width = PER * HEAD
    half = n_seq // 2
    owners = n_dp // 2
    tokens_all = n_dp * n_seq * block
    factor = 1.0 / math.sqrt(HEAD)

    def kernel(
        layout_ref, x_hbm, g_hbm, gains_hbm, out_hbm, gain_out,
        xv, gv, gains, nrm, far, rsend, rrecv, dn, scale, macc, ov,
        gg, rsbuf, zlow, zbuf, fin,
        load_sem, out_sem, g_s, g_r, f_s, f_r, r_s, r_r,
        rs_s, rs_r, zl_s, zl_r, z_s, z_r, ag_s, ag_r,
    ):
        z = lax.axis_index("seq")
        d = lax.axis_index("dp")
        s = lax.axis_index("section")
        high = z >= half
        low = z < half
        partner = lax.rem(z + half, n_seq)
        slot = lax.rem(z, half)
        owner = lax.rem(d, 2) == 0
        piece = d // 2
        below = lax.rem(s + n_section - 1, n_section)
        above = lax.rem(s + 1, n_section)

        def remote(src, dst, send, recv, where):
            return pltpu.make_async_remote_copy(
                src_ref=src, dst_ref=dst, send_sem=send, recv_sem=recv,
                device_id=where, device_id_type=MESH,
            )

        bar = pltpu.get_barrier_semaphore()

        def greet(where):
            pl.semaphore_signal(bar, inc=1, device_id=where, device_id_type=MESH)

        @pl.when(high)
        def _():
            greet({"seq": partner})

        load_x = pltpu.make_async_copy(x_hbm.at[0, 0], xv, load_sem.at[0])
        load_x.start()
        load_gains = pltpu.make_async_copy(gains_hbm.at[0], gains, load_sem.at[1])
        load_gains.start()
        greet({"section": above})

        @pl.when(high)
        def _():
            for j in range(half):
                @pl.when(z != half + j)
                def _():
                    greet({"seq": half + j})

        @pl.when(low)
        def _():
            for j in range(half):
                greet({"seq": half + j})

        for p in range(n_dp):
            if p % 2 == 0:
                @pl.when(d != p)
                def _():
                    greet({"dp": p})
            else:
                @pl.when(owner)
                def _():
                    greet({"dp": p})

        def lanes(h):
            return pl.ds(pl.multiple_of(h * HEAD, HEAD), HEAD)

        load_x.wait()
        load_gains.wait()

        def square(h, acc):
            v = xv[:, lanes(h)].astype(F32)
            return acc + v * v

        squares = lax.fori_loop(0, heads, square, jnp.zeros((block, HEAD), F32))
        mean = jnp.sum(squares, axis=1, keepdims=True) / channels
        scale[...] = jnp.broadcast_to(lax.rsqrt(mean + EPS), (block, HEAD))

        def norm(h, _):
            nrm[h] = (xv[:, lanes(h)].astype(F32) * scale[...]).astype(BF16)
            return 0

        lax.fori_loop(0, heads, norm, 0)
        macc[...] = jnp.zeros_like(macc)
        gg[...] = jnp.zeros_like(gg)

        dp_waits = jnp.where(owner, n_dp - 1, owners)
        pl.semaphore_wait(bar, jnp.where(high, 2 * half - 1, 1) + 1 + dp_waits)

        def far_copy(c):
            part = pl.ds(c * PER, PER)
            return remote(nrm.at[part], far.at[part], f_s.at[c], f_r.at[c], {"seq": partner})

        def ret_copy(c):
            part = pl.ds(c * PER, PER)
            return remote(rsend.at[part], rrecv.at[part], r_s.at[c], r_r.at[c], {"seq": partner})

        def g_copy(c):
            part = pl.ds(pl.multiple_of(c * width, width), width)
            return remote(
                g_hbm.at[0, 0, :, part], gv.at[:, part], g_s.at[c], g_r.at[c], {"section": below}
            )

        @pl.when(low)
        def _():
            def send(c, _):
                far_copy(c).start()
                return 0

            lax.fori_loop(0, chunks, send, 0)

        def send_g(c, _):
            g_copy(c).start()
            return 0

        lax.fori_loop(0, chunks, send_g, 0)

        def head(h, with_far):
            part = lanes(h)
            g0 = gains[pl.ds(0, 1), part]
            g1 = gains[pl.ds(1, 1), part]
            g2 = gains[pl.ds(2, 1), part]
            n = nrm[h].astype(F32)
            q = (n * g0).astype(BF16)
            k = (n * g1).astype(BF16)
            v = (n * g2).astype(BF16)
            cot = gv[:, part]
            key = lax.broadcasted_iota(jnp.int32, (block, block), 0)
            query = lax.broadcasted_iota(jnp.int32, (block, block), 1)
            if with_far:
                nf = far[h].astype(F32)
                k = jnp.concatenate([k, (nf * g1).astype(BF16)], axis=0)
                v = jnp.concatenate([v, (nf * g2).astype(BF16)], axis=0)
            scores = dot(k, q, ((1,), (1,))) * factor
            dprobs = dot(v, cot, ((1,), (1,)))
            near = jnp.where(key <= query, scores[:block], NEG)
            if with_far:
                usable = jnp.full((block, block), layout_ref[0, 0], jnp.int32) == 1
                scores = jnp.concatenate([near, jnp.where(usable, scores[block:], NEG)], axis=0)
            else:
                scores = near
            top = jnp.max(scores, axis=0, keepdims=True)
            weights = jnp.exp(scores - top)
            probs = weights * (1.0 / jnp.sum(weights, axis=0, keepdims=True))
            delta = jnp.sum(probs * dprobs, axis=0, keepdims=True)
            dscores = (probs * (dprobs - delta) * factor).astype(BF16)
            d_query = dot(dscores, k, ((0,), (0,)))
            d_key = dot(dscores, q, ((1,), (0,)))
            d_value = dot(probs.astype(BF16), cot, ((1,), (0,)))
            own_key, own_value = d_key[:block], d_value[:block]
            key_terms = own_key * n
            value_terms = own_value * n
            if with_far:
                far_key, far_value = d_key[block:], d_value[block:]
                key_terms += far_key * nf
                value_terms += far_value * nf
                rsend[h] = (far_key * g1 + far_value * g2).astype(BF16)
            gg[pl.ds(3 * h, 1), :] = jnp.sum(d_query * n, axis=0, keepdims=True)
            gg[pl.ds(3 * h + 1, 1), :] = jnp.sum(key_terms, axis=0, keepdims=True)
            gg[pl.ds(3 * h + 2, 1), :] = jnp.sum(value_terms, axis=0, keepdims=True)
            d_normed = d_query * g0 + own_key * g1 + own_value * g2
            dn[h] = d_normed
            return d_normed * xv[:, part].astype(F32)

        def rs_copy(p, source_slot):
            return remote(
                gg.at[pl.ds(8 * p, 8)], rsbuf.at[source_slot], rs_s.at[p], rs_r.at[source_slot],
                {"dp": 2 * p},
            )

        def rs_send():
            for p in range(owners):
                @pl.when(d != 2 * p)
                def _():
                    rs_copy(p, d).start()

                @pl.when(d == 2 * p)
                def _():
                    rsbuf[2 * p] = gg[pl.ds(8 * p, 8), :]

        def rs_sum():
            for p in range(n_dp):
                @pl.when(d != p)
                def _():
                    rs_copy(0, p).wait_recv()
            return jnp.sum(rsbuf[...], axis=0)

        def rs_wait_send():
            for p in range(owners):
                @pl.when(d != 2 * p)
                def _():
                    rs_copy(p, d).wait_send()

        zl_copy = remote(zlow.at[0], zlow.at[1], zl_s, zl_r, {"seq": partner})

        def z_copy(j, source):
            return remote(zbuf.at[source], zbuf.at[source], z_s.at[j], z_r.at[source], {"seq": j})

        def ag_copy(p, source):
            return remote(fin.at[source], fin.at[source], ag_s.at[p], ag_r.at[source], {"dp": p})

        def gather_start():
            for j in range(half):
                @pl.when(z != half + j)
                def _():
                    z_copy(0, j).wait_recv()
            fin[piece] = jnp.sum(zbuf[...], axis=0) * (1.0 / math.sqrt(tokens_all))
            for p in range(n_dp):
                @pl.when(d != p)
                def _():
                    ag_copy(p, piece).start()

        def gather_end():
            for p in range(owners):
                @pl.when(d != 2 * p)
                def _():
                    ag_copy(0, p).wait_recv()
            for h in range(heads):
                for r in range(3):
                    row = 3 * h + r
                    gain_out[0, pl.ds(r, 1), pl.ds(h * HEAD, HEAD)] = fin[
                        row // 8, pl.ds(row % 8, 1), :
                    ]

            @pl.when(owner)
            def _():
                for p in range(n_dp):
                    @pl.when(d != p)
                    def _():
                        ag_copy(p, piece).wait_send()

        def out_copy(c):
            part = pl.ds(pl.multiple_of(c * width, width), width)
            return pltpu.make_async_copy(
                ov.at[:, part], out_hbm.at[0, 0, :, part], out_sem.at[c]
            )

        def finish():
            inv = scale[...]
            total = jnp.sum(macc[...], axis=1, keepdims=True) / channels
            pull = inv * inv * inv * total

            def body(c, _):
                for i in range(PER):
                    h = c * PER + i
                    part = lanes(h)
                    ov[:, part] = (
                        gv[:, part].astype(F32) + inv * dn[h] - xv[:, part].astype(F32) * pull
                    ).astype(BF16)
                out_copy(c).start()
                return 0

            lax.fori_loop(0, chunks, body, 0)

        @pl.when(low)
        def _():
            def near(c, _):
                g_copy(c).wait_recv()
                add = head(c * PER, False)
                for i in range(1, PER):
                    add += head(c * PER + i, False)
                macc[...] += add
                return 0

            lax.fori_loop(0, chunks, near, 0)
            rs_send()

            @pl.when(owner)
            def _():
                zlow[0] = rs_sum()
                zl_copy.start()

            def back(c, _):
                ret_copy(c).wait_recv()
                for i in range(PER):
                    h = c * PER + i
                    more = rrecv[h].astype(F32)
                    dn[h] += more
                    macc[...] += more * xv[:, lanes(h)].astype(F32)
                return 0

            lax.fori_loop(0, chunks, back, 0)
            finish()

            @pl.when(owner)
            def _():
                gather_start()

            gather_end()

            @pl.when(owner)
            def _():
                zl_copy.wait_send()

            def sent(c, _):
                far_copy(c).wait_send()
                return 0

            lax.fori_loop(0, chunks, sent, 0)

        @pl.when(high)
        def _():
            def both(c, _):
                g_copy(c).wait_recv()
                far_copy(c).wait_recv()
                add = head(c * PER, True)
                for i in range(1, PER):
                    add += head(c * PER + i, True)
                ret_copy(c).start()
                macc[...] += add
                return 0

            lax.fori_loop(0, chunks, both, 0)
            rs_send()

            @pl.when(owner)
            def _():
                mine = rs_sum()
                zl_copy.wait_recv()
                zbuf[slot] = mine + zlow[1]
                for j in range(n_seq):
                    @pl.when(z != j)
                    def _():
                        z_copy(j, slot).start()
                gather_start()

            finish()
            gather_end()

            @pl.when(owner)
            def _():
                for j in range(n_seq):
                    @pl.when(z != j)
                    def _():
                        z_copy(j, slot).wait_send()

            def sent(c, _):
                ret_copy(c).wait_send()
                return 0

            lax.fori_loop(0, chunks, sent, 0)

        rs_wait_send()

        def last(c, _):
            g_copy(c).wait_send()
            out_copy(c).wait()
            return 0

        lax.fori_loop(0, chunks, last, 0)

    dma = pltpu.SemaphoreType.DMA
    scratch = [
        pltpu.VMEM((block, channels), BF16),
        pltpu.VMEM((block, channels), BF16),
        pltpu.VMEM((3, channels), F32),
        pltpu.VMEM((heads, block, HEAD), BF16),
        pltpu.VMEM((heads, block, HEAD), BF16),
        pltpu.VMEM((heads, block, HEAD), BF16),
        pltpu.VMEM((heads, block, HEAD), BF16),
        pltpu.VMEM((heads, block, HEAD), F32),
        pltpu.VMEM((block, HEAD), F32),
        pltpu.VMEM((block, HEAD), F32),
        pltpu.VMEM((block, channels), BF16),
        pltpu.VMEM((8 * owners, HEAD), F32),
        pltpu.VMEM((n_dp, 8, HEAD), F32),
        pltpu.VMEM((2, 8, HEAD), F32),
        pltpu.VMEM((half, 8, HEAD), F32),
        pltpu.VMEM((owners, 8, HEAD), F32),
        dma((2,)), dma((chunks,)),
        dma((chunks,)), dma((chunks,)), dma((chunks,)), dma((chunks,)),
        dma((chunks,)), dma((chunks,)),
        dma((owners,)), dma((n_dp,)), dma(()), dma(()),
        dma((n_seq,)), dma((half,)), dma((n_dp,)), dma((owners,)),
    ]
    return pl.pallas_call(
        kernel,
        out_shape=(
            jax.ShapeDtypeStruct((1, 1, block, channels), BF16),
            jax.ShapeDtypeStruct((1, 3, channels), F32),
        ),
        in_specs=[
            pl.BlockSpec(memory_space=pltpu.SMEM),
            pl.BlockSpec(memory_space=pl.ANY),
            pl.BlockSpec(memory_space=pl.ANY),
            pl.BlockSpec(memory_space=pl.ANY),
        ],
        out_specs=(
            pl.BlockSpec(memory_space=pl.ANY),
            pl.BlockSpec(memory_space=pltpu.VMEM),
        ),
        scratch_shapes=scratch,
        compiler_params=pltpu.CompilerParams(
            collective_id=0, has_side_effects=True, vmem_limit_bytes=32 << 20
        ),
    )


def solution(mesh):
    def local(section_inputs, grad_send, gains, layout):
        call = make_kernel(
            mesh.shape["seq"], mesh.shape["dp"], mesh.shape["section"],
            section_inputs.shape[-1], section_inputs.shape[-2],
        )
        return call(layout, section_inputs, grad_send, gains)

    in_specs = (
        P("section", "dp", "seq", None),
        P("section", "dp", "seq", None),
        P("section", None, None),
        P("section", "seq"),
    )
    out_specs = (P("section", "dp", "seq", None), P("section", None, None))
    return jax.shard_map(local, mesh=mesh, in_specs=in_specs, out_specs=out_specs, check_vma=False)
```

time: 611 us -> 73.3 us (0.12)
  blocking collectives: 486 us -> 0 us
  waiting for transfers between devices: 70.6 us -> 0 us
  Pallas kernels: 0 us -> 66.9 us
  starting transfers between devices: 26.7 us -> 0 us
  matrix products: 12.2 us -> 0 us
  other arithmetic: 7.19 us -> 0 us
    psum x1 -> x0, blocking collectives: 486 us -> none  [local(): summed = lax.psum(terms, ('seq', 'dp'))]
    ppermute x5 -> x0, waiting for transfers between devices: 70.6 us -> none  [the longest x4 70.6 us: from_behind(): lax.ppermute(value, axis, [(source, source + steps) for source in range(i...]
    pallas_call x0 -> x1, Pallas kernels: none -> 66.9 us  [local(): return call(layout, section_inputs, grad_send, gains)]
    ppermute x5 -> x0, starting transfers between devices: 26.7 us -> none  [the longest x4 19.8 us: from_behind(): lax.ppermute(value, axis, [(source, source + steps) for source in range(i...]
    dot_general x10 -> x0, matrix products: 12.2 us -> none  [contract(): return jnp.einsum(form, left, right, preferred_element_type=jnp.float32)]
  transfers between devices with their start and end apart: 5 -> 0, of which waited for: 4 -> 0; matrix products, arithmetic and copies ran while one was open for 2% -> 0% of each run, Pallas kernels for 0% -> 0%
where the time goes in v1:
time: 73.3 us; the launch traced here: 72.6 us
  Pallas kernels  66.9 us (91%)
  local copies, waits for them, and re-layouts  4.41 us (6%)
  between operations  1.3 us (2%)
    pallas_call x1, Pallas kernels, local(): return call(layout, section_inputs, grad_send, gains)  66.9 us
    unnamed x6, local copies, waits for them, and re-layouts  3.77 us

profile of v1, /device:TPU:1, one launch (start us, length us, event | category | flops | bytes accessed | tf_op | source)
XLA Modules:
  0.0 72.6 jit_solution(4698580982365974051)
XLA Ops:
  1.3 0.8 %copy.6.gains_hbm = f32[1,3,2560]{2,1,0:T(4,128)S(1)} copy(f32[1,3,2560]{2,0,1:T(1,128)} %param.6) | data formatting | bytes 61440 | tf_op args[2]
  2.0 0.0 copy-start
  2.1 1.1 %copy-done = bf16[1,1,128,2560]{3,2,1,0:T(8,128)(2,1)S(1)} copy-done((bf16[1,1,128,2560]{3,2,1,0:T(8,128)(2,1)S(1)}, bf16[1,1,128,2560]{3,2,1,0:T(8,128)(2,1)}, u32[]{:S(2)}) %copy-start) | copy-done | bytes 655384
  3.1 0.0 copy-start.1
  3.1 1.1 %copy-done.1 = bf16[1,1,128,2560]{3,2,1,0:T(8,128)(2,1)S(1)} copy-done((bf16[1,1,128,2560]{3,2,1,0:T(8,128)(2,1)S(1)}, bf16[1,1,128,2560]{3,2,1,0:T(8,128)(2,1)}, u32[]{:S(2)}) %copy-start.1) | copy-done | bytes 655384
  4.2 66.9 %shard_map.59 = (bf16[1,1,128,2560]{3,2,1,0:T(8,128)(2,1)S(1)}, f32[1,3,2560]{2,1,0:T(4,128)S(1)}) custom-call(s32[1,1]{1,0:T(1,128)S(6)} %copy.9.layout_ref, bf16[1,1,128,2560]{3,2,1,0:T(8,128)(2,1)S(1)} %copy-done, bf16[1,1,128,2560]{3,2,1,0:T(8,128)(2,1)S(1)} %copy-done.1, f32[1,3,2560]{2,1,0:T(4,128)S(1)} %copy.6.gains_hbm), custom_call_target="tpu_custom_call" | custom-call | tf_op jit(solution)/shard_map/pallas_call | solution.py:434
  71.1 0.6 copy.7
  71.8 0.8 %copy.10 = bf16[1,1,128,2560]{3,2,1,0:T(8,128)(2,1)} copy(bf16[1,1,128,2560]{3,2,1,0:T(8,128)(2,1)S(1)} %get-tuple-element.6) | data formatting | bytes 1310720
Async XLA Ops:
  2.0 1.1 %copy-start = (bf16[1,1,128,2560]{3,2,1,0:T(8,128)(2,1)S(1)}, bf16[1,1,128,2560]{3,2,1,0:T(8,128)(2,1)}, u32[]{:S(2)}) copy-start(bf16[1,1,128,2560]{3,2,1,0:T(8,128)(2,1)} %x_hbm.1) | copy-start | bytes 1966084
  3.1 1.1 %copy-start.1 = (bf16[1,1,128,2560]{3,2,1,0:T(8,128)(2,1)S(1)}, bf16[1,1,128,2560]{3,2,1,0:T(8,128)(2,1)}, u32[]{:S(2)}) copy-start(bf16[1,1,128,2560]{3,2,1,0:T(8,128)(2,1)} %g_hbm.1) | copy-start | bytes 1966084

commit v2 on v1

v2 whole, which is shorter than its diff:
```python
import math

import jax
import jax.numpy as jnp
from jax import lax
from jax.experimental import pallas as pl
from jax.experimental.pallas import tpu as pltpu
from jax.sharding import PartitionSpec as P

MESH = pl.DeviceIdType.MESH
HEAD = 128
EPS = 1e-06
NEG = -1e30
PER = 2
FORWARD = 8
GROUPS = ((0, 4), (4, 7), (7, 8), (0, 8), (8, 10))
HIGH_GROUPS, LOW_GROUPS = (0, 1, 2), (3, 4)
F32 = jnp.float32
BF16 = jnp.bfloat16


def dot(left, right, dims):
    return lax.dot_general(left, right, (dims, ((), ())), preferred_element_type=F32)


def make_kernel(n_seq, n_dp, n_section, channels, block):
    heads = channels // HEAD
    chunks = heads // PER
    moved = chunks - FORWARD
    width = PER * HEAD
    half = n_seq // 2
    chips = n_dp // 2
    groups = len(GROUPS)
    tokens_all = n_dp * n_seq * block
    factor = 1.0 / math.sqrt(HEAD)

    def kernel(
        layout_hbm, x_hbm, g_hbm, gains_hbm, out_hbm, gain_out,
        layout, xv, gv, gains, nrm, far, rsend, rrecv, nq, gq, msend, mrecv, flag,
        dn, scale, macc, ov, gg, zbuf, pair, xbuf, fin,
        load_sem, out_sem, g_s, g_r, f_s, f_r, r_s, r_r,
        nq_s, nq_r, gq_s, gq_r, m_s, m_r, one_s, one_r, z_s, z_r, sib_s, sib_r, x_s, x_r,
    ):
        z = lax.axis_index("seq")
        d = lax.axis_index("dp")
        s = lax.axis_index("section")
        high = z >= half
        low = z < half
        partner = lax.rem(z + half, n_seq)
        chip = d // 2
        core = lax.rem(d, 2)
        sibling = 2 * chip + 1 - core
        below = lax.rem(s + n_section - 1, n_section)
        above = lax.rem(s + 1, n_section)

        def remote(src, dst, send, recv, where):
            return pltpu.make_async_remote_copy(
                src_ref=src, dst_ref=dst, send_sem=send, recv_sem=recv,
                device_id=where, device_id_type=MESH,
            )

        bar = pltpu.get_barrier_semaphore()

        def greet(where):
            pl.semaphore_signal(bar, inc=1, device_id=where, device_id_type=MESH)

        greet({"seq": partner})
        load_x = pltpu.make_async_copy(x_hbm.at[0, 0], xv, load_sem.at[0])
        load_x.start()
        load_gains = pltpu.make_async_copy(gains_hbm, gains, load_sem.at[1])
        load_gains.start()
        load_layout = pltpu.make_async_copy(layout_hbm, layout, load_sem.at[2])
        load_layout.start()
        greet({"section": above})
        greet({"dp": sibling})
        for p in range(chips):
            @pl.when(chip != p)
            def _():
                greet({"dp": 2 * p + core})

        @pl.when(low)
        def _():
            greet({"section": above, "seq": partner})
            for j in range(half):
                @pl.when(z != j)
                def _():
                    greet({"seq": j})
                    greet({"seq": half + j})

        def lanes(h):
            return pl.ds(pl.multiple_of(h * HEAD, HEAD), HEAD)

        def wide(c):
            return pl.ds(pl.multiple_of(c * width, width), width)

        load_x.wait()

        def square(h, acc):
            v = xv[:, lanes(h)].astype(F32)
            return acc + v * v

        squares = lax.fori_loop(0, heads, square, jnp.zeros((block, HEAD), F32))
        mean = jnp.sum(squares, axis=1, keepdims=True) / channels
        scale[...] = jnp.broadcast_to(lax.rsqrt(mean + EPS), (block, HEAD))

        def norm(h, _):
            nrm[h] = (xv[:, lanes(h)].astype(F32) * scale[...]).astype(BF16)
            return 0

        lax.fori_loop(0, heads, norm, 0)
        load_gains.wait()
        load_layout.wait()
        flag[0] = jnp.full((8, HEAD), layout[0, 0], jnp.int32).astype(F32)
        macc[...] = jnp.zeros_like(macc)
        gg[...] = jnp.zeros_like(gg)

        pl.semaphore_wait(bar, jnp.where(high, half + 2, half + 1) + chips)

        def far_copy(c):
            part = pl.ds(c * PER, PER)
            return remote(nrm.at[part], far.at[part], f_s.at[c], f_r.at[c], {"seq": partner})

        def ret_copy(c):
            part = pl.ds(c * PER, PER)
            return remote(rsend.at[part], rrecv.at[part], r_s.at[c], r_r.at[c], {"seq": partner})

        def nq_copy(m):
            return remote(
                nrm.at[pl.ds((FORWARD + m) * PER, PER)], nq.at[pl.ds(m * PER, PER)],
                nq_s.at[m], nq_r.at[m], {"seq": partner},
            )

        def gq_copy(m):
            return remote(
                g_hbm.at[0, 0, :, wide(FORWARD + m)], gq.at[:, wide(m)],
                gq_s.at[m], gq_r.at[m], {"section": below, "seq": partner},
            )

        def back_copy(m):
            part = pl.ds(m * PER, PER)
            return remote(msend.at[part], mrecv.at[part], m_s.at[m], m_r.at[m], {"seq": partner})

        def g_copy(c):
            part = wide(c)
            return remote(
                g_hbm.at[0, 0, :, part], gv.at[:, part], g_s.at[c], g_r.at[c], {"section": below}
            )

        flag_copy = remote(flag.at[0], flag.at[1], one_s.at[0], one_r.at[0], {"seq": partner})
        total_copy = remote(fin, fin, one_s.at[1], one_r.at[1], {"seq": partner})

        @pl.when(low)
        def _():
            def send(c, _):
                far_copy(c).start()
                return 0

            lax.fori_loop(0, FORWARD, send, 0)

        @pl.when(high)
        def _():
            flag_copy.start()

            def send(m, _):
                nq_copy(m).start()
                gq_copy(m).start()
                return 0

            lax.fori_loop(0, moved, send, 0)

        def send_g(c, _):
            g_copy(c).start()
            return 0

        lax.fori_loop(0, chunks, send_g, 0)

        def head(h, own, cot, other=None, flags=None):
            part = lanes(h)
            g0 = gains[0, :, part]
            g1 = gains[1, :, part]
            g2 = gains[2, :, part]
            n = own.astype(F32)
            q = (n * g0).astype(BF16)
            k = (n * g1).astype(BF16)
            v = (n * g2).astype(BF16)
            key = lax.broadcasted_iota(jnp.int32, (block, block), 0)
            query = lax.broadcasted_iota(jnp.int32, (block, block), 1)
            if other is not None:
                nf = other.astype(F32)
                k = jnp.concatenate([k, (nf * g1).astype(BF16)], axis=0)
                v = jnp.concatenate([v, (nf * g2).astype(BF16)], axis=0)
            scores = dot(k, q, ((1,), (1,))) * factor
            dprobs = dot(v, cot, ((1,), (1,)))
            near = jnp.where(key <= query, scores[:block], NEG)
            if other is not None:
                scores = jnp.concatenate([near, jnp.where(flags > 0.5, scores[block:], NEG)], axis=0)
            else:
                scores = near
            top = jnp.max(scores, axis=0, keepdims=True)
            weights = jnp.exp(scores - top)
            probs = weights * (1.0 / jnp.sum(weights, axis=0, keepdims=True))
            delta = jnp.sum(probs * dprobs, axis=0, keepdims=True)
            dscores = (probs * (dprobs - delta) * factor).astype(BF16)
            d_query = dot(dscores, k, ((0,), (0,)))
            d_key = dot(dscores, q, ((1,), (0,)))
            d_value = dot(probs.astype(BF16), cot, ((1,), (0,)))
            own_key, own_value = d_key[:block], d_value[:block]
            key_terms = own_key * n
            value_terms = own_value * n
            d_far = None
            if other is not None:
                far_key, far_value = d_key[block:], d_value[block:]
                key_terms += far_key * nf
                value_terms += far_value * nf
                d_far = far_key * g1 + far_value * g2
            sums = [
                jnp.sum(term, axis=0, keepdims=True) for term in (d_query * n, key_terms, value_terms)
            ]
            return d_query * g0 + own_key * g1 + own_value * g2, d_far, sums

        def put_sums(c, i, sums):
            for r in range(3):
                gg[c, pl.ds(3 * i + r, 1), :] = sums[r]

        def x_of(h):
            return xv[:, lanes(h)].astype(F32)

        def tiles_of(k):
            return pl.ds(GROUPS[k][0], GROUPS[k][1] - GROUPS[k][0])

        def sib_copy(k):
            part = tiles_of(k)
            return remote(gg.at[part], pair.at[part], sib_s.at[k], sib_r.at[k], {"dp": sibling})

        def x_copy(k, p, source):
            part = tiles_of(k)
            return remote(
                xbuf.at[source, part], xbuf.at[source, part],
                x_s.at[k, p], x_r.at[k, source], {"dp": 2 * p + core},
            )

        def z_copy(k, j, source):
            part = tiles_of(k)
            return remote(
                zbuf.at[source, part], zbuf.at[source, part],
                z_s.at[k, j], z_r.at[k, source], {"seq": j},
            )

        def over_cores(k):
            part = tiles_of(k)
            sib_copy(k).wait_recv()
            xbuf[chip, part] = gg[part] + pair[part]
            for p in range(chips):
                @pl.when(chip != p)
                def _():
                    x_copy(k, p, chip).start()

        def over_x(k):
            part = tiles_of(k)
            for p in range(chips):
                @pl.when(chip != p)
                def _():
                    x_copy(k, 0, p).wait_recv()
            zbuf[z, part] = jnp.sum(xbuf[:, part], axis=0)
            for j in range(half):
                @pl.when(z != j)
                def _():
                    z_copy(k, j, z).start()

        def over_z():
            for k in HIGH_GROUPS:
                for j in range(half, n_seq):
                    z_copy(k, 0, j).wait_recv()
            for k in LOW_GROUPS:
                for j in range(half):
                    @pl.when(z != j)
                    def _():
                        z_copy(k, 0, j).wait_recv()
            ratio = 1.0 / math.sqrt(tokens_all)
            fin[pl.ds(0, FORWARD)] = jnp.sum(zbuf[:, pl.ds(0, FORWARD)], axis=0) * ratio
            fin[pl.ds(FORWARD, moved)] = (
                jnp.sum(zbuf[pl.ds(0, half), pl.ds(FORWARD, moved)], axis=0) * ratio
            )

        def sums_sent(k):
            sib_copy(k).wait_send()
            for p in range(chips):
                @pl.when(chip != p)
                def _():
                    x_copy(k, p, chip).wait_send()
            for j in range(half):
                @pl.when(z != j)
                def _():
                    z_copy(k, j, z).wait_send()

        def write_gains():
            for c in range(chunks):
                for i in range(PER):
                    for r in range(3):
                        part = pl.ds((c * PER + i) * HEAD, HEAD)
                        gain_out[r, :, part] = fin[c, pl.ds(3 * i + r, 1), :]

        def out_copy(c):
            part = wide(c)
            return pltpu.make_async_copy(
                ov.at[:, part], out_hbm.at[0, 0, :, part], out_sem.at[c]
            )

        def finish():
            inv = scale[...]
            total = jnp.sum(macc[...], axis=1, keepdims=True) / channels
            pull = inv * inv * inv * total

            def body(c, _):
                for i in range(PER):
                    h = c * PER + i
                    part = lanes(h)
                    ov[:, part] = (
                        gv[:, part].astype(F32) + inv * dn[h] - x_of(h) * pull
                    ).astype(BF16)
                out_copy(c).start()
                return 0

            lax.fori_loop(0, chunks, body, 0)

        @pl.when(low)
        def _():
            def near(c, _):
                g_copy(c).wait_recv()
                add = macc[...]
                for i in range(PER):
                    h = c * PER + i
                    grad, _far, sums = head(h, nrm[h], gv[:, lanes(h)])
                    dn[h] = grad
                    put_sums(c, i, sums)
                    add += grad * x_of(h)
                macc[...] = add
                return 0

            lax.fori_loop(0, chunks, near, 0)
            sib_copy(LOW_GROUPS[0]).start()
            flag_copy.wait_recv()

            def mine(m, _):
                nq_copy(m).wait_recv()
                gq_copy(m).wait_recv()
                add = macc[...]
                c = FORWARD + m
                for i in range(PER):
                    h = c * PER + i
                    grad, d_far, sums = head(
                        h, nq[m * PER + i], gq[:, lanes(m * PER + i)], nrm[h], flag[1, pl.ds(0, 1), :]
                    )
                    msend[m * PER + i] = grad.astype(BF16)
                    dn[h] += d_far
                    put_sums(c, i, [gg[c, pl.ds(3 * i + r, 1), :] + sums[r] for r in range(3)])
                    add += d_far * x_of(h)
                back_copy(m).start()
                macc[...] = add
                return 0

            lax.fori_loop(0, moved, mine, 0)
            sib_copy(LOW_GROUPS[1]).start()
            for k in LOW_GROUPS:
                over_cores(k)
            for k in LOW_GROUPS:
                over_x(k)

            def back(c, _):
                ret_copy(c).wait_recv()
                add = macc[...]
                for i in range(PER):
                    h = c * PER + i
                    more = rrecv[h].astype(F32)
                    dn[h] += more
                    add += more * x_of(h)
                macc[...] = add
                return 0

            lax.fori_loop(0, FORWARD, back, 0)
            finish()
            over_z()
            total_copy.start()
            write_gains()

            def sent(c, _):
                far_copy(c).wait_send()
                return 0

            lax.fori_loop(0, FORWARD, sent, 0)

            def given(m, _):
                back_copy(m).wait_send()
                return 0

            lax.fori_loop(0, moved, given, 0)
            for k in LOW_GROUPS:
                sums_sent(k)
            total_copy.wait_send()

        @pl.when(high)
        def _():
            def both(c, _):
                g_copy(c).wait_recv()
                far_copy(c).wait_recv()
                add = macc[...]
                for i in range(PER):
                    h = c * PER + i
                    grad, d_far, sums = head(
                        h, nrm[h], gv[:, lanes(h)], far[h], flag[0, pl.ds(0, 1), :]
                    )
                    dn[h] = grad
                    rsend[h] = d_far.astype(BF16)
                    put_sums(c, i, sums)
                    add += grad * x_of(h)
                ret_copy(c).start()
                macc[...] = add

                @pl.when(c == GROUPS[0][1] - 1)
                def _():
                    sib_copy(0).start()

                @pl.when(c == GROUPS[0][1])
                def _():
                    over_cores(0)

                @pl.when(c == GROUPS[1][1] - 1)
                def _():
                    sib_copy(1).start()

                return 0

            lax.fori_loop(0, FORWARD, both, 0)
            sib_copy(2).start()
            over_cores(1)
            over_cores(2)
            for k in HIGH_GROUPS:
                over_x(k)

            def theirs(m, _):
                back_copy(m).wait_recv()
                g_copy(FORWARD + m).wait_recv()
                add = macc[...]
                for i in range(PER):
                    h = (FORWARD + m) * PER + i
                    grad = mrecv[m * PER + i].astype(F32)
                    dn[h] = grad
                    add += grad * x_of(h)
                macc[...] = add
                return 0

            lax.fori_loop(0, moved, theirs, 0)
            finish()
            total_copy.wait_recv()
            write_gains()

            def sent(c, _):
                ret_copy(c).wait_send()
                return 0

            lax.fori_loop(0, FORWARD, sent, 0)

            def given(m, _):
                nq_copy(m).wait_send()
                gq_copy(m).wait_send()
                return 0

            lax.fori_loop(0, moved, given, 0)
            flag_copy.wait_send()
            for k in HIGH_GROUPS:
                sums_sent(k)

        def last(c, _):
            g_copy(c).wait_send()
            out_copy(c).wait()
            return 0

        lax.fori_loop(0, chunks, last, 0)

    dma = pltpu.SemaphoreType.DMA
    whole = pltpu.VMEM((heads, block, HEAD), BF16)
    some = pltpu.VMEM((moved * PER, block, HEAD), BF16)
    tiles = (chunks, 8, HEAD)
    scratch = [
        pltpu.SMEM((1, 1), jnp.int32),
        pltpu.VMEM((block, channels), BF16),
        pltpu.VMEM((block, channels), BF16),
        pltpu.VMEM((3, 1, channels), F32),
        whole, whole, whole, whole,
        some,
        pltpu.VMEM((block, moved * width), BF16),
        some, some,
        pltpu.VMEM((2, 8, HEAD), F32),
        pltpu.VMEM((heads, block, HEAD), F32),
        pltpu.VMEM((block, HEAD), F32),
        pltpu.VMEM((block, HEAD), F32),
        pltpu.VMEM((block, channels), BF16),
        pltpu.VMEM(tiles, F32),
        pltpu.VMEM((n_seq, *tiles), F32),
        pltpu.VMEM(tiles, F32),
        pltpu.VMEM((chips, *tiles), F32),
        pltpu.VMEM(tiles, F32),
        dma((3,)), dma((chunks,)),
        dma((chunks,)), dma((chunks,)), dma((chunks,)), dma((chunks,)),
        dma((chunks,)), dma((chunks,)),
        dma((moved,)), dma((moved,)), dma((moved,)), dma((moved,)), dma((moved,)), dma((moved,)),
        dma((2,)), dma((2,)),
        dma((groups, half)), dma((groups, n_seq)), dma((groups,)), dma((groups,)),
        dma((groups, chips)), dma((groups, chips)),
    ]
    return pl.pallas_call(
        kernel,
        out_shape=(
            jax.ShapeDtypeStruct((1, 1, block, channels), BF16),
            jax.ShapeDtypeStruct((3, 1, channels), F32),
        ),
        in_specs=[pl.BlockSpec(memory_space=pltpu.HBM)] * 4,
        out_specs=(
            pl.BlockSpec(memory_space=pl.ANY),
            pl.BlockSpec(memory_space=pltpu.VMEM),
        ),
        scratch_shapes=scratch,
        compiler_params=pltpu.CompilerParams(
            collective_id=0, has_side_effects=True, vmem_limit_bytes=32 << 20
        ),
    )


def solution(mesh):
    def local(section_inputs, grad_send, gains, layout):
        call = make_kernel(
            mesh.shape["seq"], mesh.shape["dp"], mesh.shape["section"],
            section_inputs.shape[-1], section_inputs.shape[-2],
        )
        operands = [section_inputs, grad_send, jnp.swapaxes(gains, 0, 1)]
        operands = [pltpu.with_memory_space_constraint(v, pltpu.HBM) for v in operands]
        input_grad, gain_rows = call(layout, *operands)
        return input_grad, jnp.swapaxes(gain_rows, 0, 1)

    in_specs = (
        P("section", "dp", "seq", None),
        P("section", "dp", "seq", None),
        P("section", None, None),
        P("section", "seq"),
    )
    out_specs = (P("section", "dp", "seq", None), P("section", None, None))
    return jax.shard_map(local, mesh=mesh, in_specs=in_specs, out_specs=out_specs, check_vma=False)
```

time: 73.3 us -> 66.5 us (0.907)
  Pallas kernels: 66.9 us -> 62.8 us
  local copies, waits for them, and re-layouts: 4.41 us -> 1.45 us
    pallas_call x1, Pallas kernels: 66.9 us -> 62.8 us  [local(): input_grad, gain_rows = call(layout, *operands)]
    unnamed x6 -> x2, local copies, waits for them, and re-layouts: 3.77 us -> 1.45 us
where the time goes in v2:
time: 66.5 us; the launch traced here: 65.5 us
  Pallas kernels  62.8 us (94%)
  local copies, waits for them, and re-layouts  1.45 us (2%)
  between operations  1.29 us (2%)
    pallas_call x1, Pallas kernels, local(): input_grad, gain_rows = call(layout, *operands)  62.8 us
    unnamed x2, local copies, waits for them, and re-layouts  1.45 us

profile of v2, /device:TPU:1, one launch (start us, length us, event | category | flops | bytes accessed | tf_op | source)
XLA Modules:
  0.0 65.5 jit_solution(17612002133236679393)
XLA Ops:
  1.3 62.8 %shard_map.59 = (bf16[1,1,128,2560]{3,2,1,0:T(8,128)(2,1)S(1)}, f32[3,1,2560]{2,1,0:T(1,128)S(1)}) custom-call(s32[1,1]{1,0:T(1,128)S(6)} %copy.8.layout_hbm, bf16[1,1,128,2560]{3,2,1,0:T(8,128)(2,1)} %x_hbm.1, bf16[1,1,128,2560]{3,2,1,0:T(8,128)(2,1)} %g_hbm.1, f32[3,1,2560]{2,1,0:T(1,128)} %bitcast.3), custom_call_target="tpu_custom_call" | custom-call | tf_op jit(solution)/shard_map/pallas_call | solution.py:537
  64.1 0.8 %copy.9 = bf16[1,1,128,2560]{3,2,1,0:T(8,128)(2,1)} copy(bf16[1,1,128,2560]{3,2,1,0:T(8,128)(2,1)S(1)} %get-tuple-element.8) | data formatting | bytes 1310720
  64.9 0.6 copy.10

commit v3 on v2

--- a/solution.py
+++ b/solution.py
@@ -13,7 +13,7 @@
 NEG = -1e30
 PER = 2
 FORWARD = 8
-GROUPS = ((0, 4), (4, 7), (7, 8), (0, 8), (8, 10))
+GROUPS = ((0, 5), (5, 7), (7, 8), (0, 8), (8, 10))
 HIGH_GROUPS, LOW_GROUPS = (0, 1, 2), (3, 4)
 F32 = jnp.float32
 BF16 = jnp.bfloat16
@@ -39,7 +39,7 @@
         layout, xv, gv, gains, nrm, far, rsend, rrecv, nq, gq, msend, mrecv, flag,
         dn, scale, macc, ov, gg, zbuf, pair, xbuf, fin,
         load_sem, out_sem, g_s, g_r, f_s, f_r, r_s, r_r,
-        nq_s, nq_r, gq_s, gq_r, m_s, m_r, one_s, one_r, z_s, z_r, sib_s, sib_r, x_s, x_r,
+        nq_s, nq_r, gq_s, gq_r, m_s, m_r, one_s, one_r, z_s, z_r, sib_s, sib_r, x_s, x_r, up, go,
     ):
         z = lax.axis_index("seq")
         d = lax.axis_index("dp")
@@ -72,11 +72,14 @@
         load_layout = pltpu.make_async_copy(layout_hbm, layout, load_sem.at[2])
         load_layout.start()
         greet({"section": above})
-        greet({"dp": sibling})
-        for p in range(chips):
-            @pl.when(chip != p)
-            def _():
-                greet({"dp": 2 * p + core})
+
+        @pl.when(low & (z != 0))
+        def _():
+            greet({"dp": sibling})
+            for p in range(chips):
+                @pl.when(chip != p)
+                def _():
+                    greet({"dp": 2 * p + core})
 
         @pl.when(low)
         def _():
@@ -114,7 +117,7 @@
         macc[...] = jnp.zeros_like(macc)
         gg[...] = jnp.zeros_like(gg)
 
-        pl.semaphore_wait(bar, jnp.where(high, half + 2, half + 1) + chips)
+        pl.semaphore_wait(bar, jnp.where(high, half + 2, jnp.where(z == 0, half + 1, half + 1 + chips)))
 
         def far_copy(c):
             part = pl.ds(c * PER, PER)
@@ -147,7 +150,23 @@
             )
 
         flag_copy = remote(flag.at[0], flag.at[1], one_s.at[0], one_r.at[0], {"seq": partner})
-        total_copy = remote(fin, fin, one_s.at[1], one_r.at[1], {"seq": partner})
+
+        def total_copy(i, part):
+            return remote(
+                fin.at[part], fin.at[part], one_s.at[1 + i], one_r.at[1 + i], {"seq": partner}
+            )
+
+        def tell_peers():
+            pl.semaphore_signal(up, inc=1, device_id={"dp": sibling}, device_id_type=MESH)
+            for p in range(chips):
+                @pl.when(chip != p)
+                def _():
+                    pl.semaphore_signal(
+                        up, inc=1, device_id={"dp": 2 * p + core}, device_id_type=MESH
+                    )
+
+        def tell(where):
+            pl.semaphore_signal(go, inc=1, device_id={"seq": where}, device_id_type=MESH)
 
         @pl.when(low)
         def _():
@@ -156,6 +175,10 @@
                 return 0
 
             lax.fori_loop(0, FORWARD, send, 0)
+
+        @pl.when(low & (z != 0))
+        def _():
+            tell_peers()
 
         @pl.when(high)
         def _():
@@ -267,8 +290,14 @@
                 def _():
                     z_copy(k, j, z).start()
 
+        late = tiles_of(HIGH_GROUPS[-1])
+
+        def add_up(part, sources):
+            ratio = 1.0 / math.sqrt(tokens_all)
+            fin[part] = jnp.sum(zbuf[pl.ds(0, sources), part], axis=0) * ratio
+
         def over_z():
-            for k in HIGH_GROUPS:
+            for k in HIGH_GROUPS[:-1]:
                 for j in range(half, n_seq):
                     z_copy(k, 0, j).wait_recv()
             for k in LOW_GROUPS:
@@ -276,11 +305,19 @@
                     @pl.when(z != j)
                     def _():
                         z_copy(k, 0, j).wait_recv()
-            ratio = 1.0 / math.sqrt(tokens_all)
-            fin[pl.ds(0, FORWARD)] = jnp.sum(zbuf[:, pl.ds(0, FORWARD)], axis=0) * ratio
-            fin[pl.ds(FORWARD, moved)] = (
-                jnp.sum(zbuf[pl.ds(0, half), pl.ds(FORWARD, moved)], axis=0) * ratio
-            )
+            add_up(pl.ds(0, GROUPS[HIGH_GROUPS[-1]][0]), n_seq)
+            add_up(pl.ds(FORWARD, moved), half)
+            total_copy(0, pl.ds(0, GROUPS[HIGH_GROUPS[-1]][0])).start()
+            total_copy(1, pl.ds(FORWARD, moved)).start()
+            for j in range(half, n_seq):
+                z_copy(HIGH_GROUPS[-1], 0, j).wait_recv()
+            add_up(late, n_seq)
+            total_copy(2, late).start()
+
+        def totals(act):
+            act(total_copy(0, pl.ds(0, GROUPS[HIGH_GROUPS[-1]][0])))
+            act(total_copy(1, pl.ds(FORWARD, moved)))
+            act(total_copy(2, late))
 
         def sums_sent(k):
             sib_copy(k).wait_send()
@@ -327,6 +364,26 @@
         def _():
             def near(c, _):
                 g_copy(c).wait_recv()
+
+                @pl.when((z != 0) & (c == 2))
+                def _():
+                    pl.semaphore_wait(up, chips)
+                    tell(partner)
+
+                @pl.when((z == 1) & (c == 2))
+                def _():
+                    tell(0)
+
+                @pl.when((z == 0) & (c == 4))
+                def _():
+                    pl.semaphore_wait(go, 1)
+                    tell_peers()
+
+                @pl.when((z == 0) & (c == 7))
+                def _():
+                    pl.semaphore_wait(up, chips)
+                    tell(partner)
+
                 add = macc[...]
                 for i in range(PER):
                     h = c * PER + i
@@ -357,12 +414,16 @@
                     add += d_far * x_of(h)
                 back_copy(m).start()
                 macc[...] = add
+
+                @pl.when(m == 0)
+                def _():
+                    over_cores(LOW_GROUPS[0])
+
                 return 0
 
             lax.fori_loop(0, moved, mine, 0)
             sib_copy(LOW_GROUPS[1]).start()
-            for k in LOW_GROUPS:
-                over_cores(k)
+            over_cores(LOW_GROUPS[1])
             for k in LOW_GROUPS:
                 over_x(k)
 
@@ -380,7 +441,6 @@
             lax.fori_loop(0, FORWARD, back, 0)
             finish()
             over_z()
-            total_copy.start()
             write_gains()
 
             def sent(c, _):
@@ -396,11 +456,18 @@
             lax.fori_loop(0, moved, given, 0)
             for k in LOW_GROUPS:
                 sums_sent(k)
-            total_copy.wait_send()
+            totals(lambda copy: copy.wait_send())
 
         @pl.when(high)
         def _():
+            first = z == half
+
             def both(c, _):
+                for k in HIGH_GROUPS[:-1]:
+                    @pl.when(~first & (c == GROUPS[k][1]))
+                    def _():
+                        over_cores(k)
+
                 g_copy(c).wait_recv()
                 far_copy(c).wait_recv()
                 add = macc[...]
@@ -416,24 +483,33 @@
                 ret_copy(c).start()
                 macc[...] = add
 
-                @pl.when(c == GROUPS[0][1] - 1)
-                def _():
+                @pl.when(~first & (c == GROUPS[0][1] - 1))
+                def _():
+                    pl.semaphore_wait(go, 1)
                     sib_copy(0).start()
 
-                @pl.when(c == GROUPS[0][1])
-                def _():
-                    over_cores(0)
-
-                @pl.when(c == GROUPS[1][1] - 1)
+                @pl.when(~first & (c == GROUPS[1][1] - 1))
                 def _():
                     sib_copy(1).start()
 
                 return 0
 
             lax.fori_loop(0, FORWARD, both, 0)
+
+            @pl.when(first)
+            def _():
+                pl.semaphore_wait(go, 1)
+                for k in HIGH_GROUPS[:-1]:
+                    sib_copy(k).start()
+
             sib_copy(2).start()
-            over_cores(1)
             over_cores(2)
+
+            @pl.when(first)
+            def _():
+                for k in HIGH_GROUPS[:-1]:
+                    over_cores(k)
+
             for k in HIGH_GROUPS:
                 over_x(k)
 
@@ -451,7 +527,7 @@
 
             lax.fori_loop(0, moved, theirs, 0)
             finish()
-            total_copy.wait_recv()
+            totals(lambda copy: copy.wait_recv())
             write_gains()
 
             def sent(c, _):
@@ -504,9 +580,10 @@
         dma((chunks,)), dma((chunks,)), dma((chunks,)), dma((chunks,)),
         dma((chunks,)), dma((chunks,)),
         dma((moved,)), dma((moved,)), dma((moved,)), dma((moved,)), dma((moved,)), dma((moved,)),
-        dma((2,)), dma((2,)),
+        dma((4,)), dma((4,)),
         dma((groups, half)), dma((groups, n_seq)), dma((groups,)), dma((groups,)),
         dma((groups, chips)), dma((groups, chips)),
+        pltpu.SemaphoreType.REGULAR, pltpu.SemaphoreType.REGULAR,
     ]
     return pl.pallas_call(
         kernel,

time: 66.5 us -> 64.3 us (0.967); the launches traced: 65.5 us -> 64.1 us
  Pallas kernels: 62.8 us -> 61.4 us
    pallas_call x1, Pallas kernels: 62.8 us -> 61.4 us  [local(): input_grad, gain_rows = call(layout, *operands)]
where the time goes in v3:
time: 64.3 us; the launch traced here: 64.1 us
  Pallas kernels  61.4 us (95%)
  local copies, waits for them, and re-layouts  1.45 us (2%)
  between operations  1.29 us (2%)
    pallas_call x1, Pallas kernels, local(): input_grad, gain_rows = call(layout, *operands)  61.4 us
    unnamed x2, local copies, waits for them, and re-layouts  1.45 us

profile of v3, /device:TPU:1, one launch (start us, length us, event | category | flops | bytes accessed | tf_op | source)
XLA Modules:
  0.0 64.1 jit_solution(4983656028375433702)
XLA Ops:
  1.3 61.4 %shard_map.59 = (bf16[1,1,128,2560]{3,2,1,0:T(8,128)(2,1)S(1)}, f32[3,1,2560]{2,1,0:T(1,128)S(1)}) custom-call(s32[1,1]{1,0:T(1,128)S(6)} %copy.8.layout_hbm, bf16[1,1,128,2560]{3,2,1,0:T(8,128)(2,1)} %x_hbm.1, bf16[1,1,128,2560]{3,2,1,0:T(8,128)(2,1)} %g_hbm.1, f32[3,1,2560]{2,1,0:T(1,128)} %bitcast.3), custom_call_target="tpu_custom_call" | custom-call | tf_op jit(solution)/shard_map/pallas_call | solution.py:614
  62.7 0.8 %copy.9 = bf16[1,1,128,2560]{3,2,1,0:T(8,128)(2,1)} copy(bf16[1,1,128,2560]{3,2,1,0:T(8,128)(2,1)S(1)} %get-tuple-element.8) | data formatting | bytes 1310720
  63.5 0.6 copy.10
